TPU v7x, 32 devices: a whole 2x2x4 slice. The times are simulated.
32 devices in a mesh: depth: 4 (over y, x), view: 8 (over z, core).
Axes of the slice: x: 2, y: 2, z: 4, core: 2. Of those that a mesh axis runs over, the one named last changes fastest.
Arguments:
- bricks: float32 [4, 8, 8, 64, 4096], P('depth', 'view'), may hold values from -6 to 6
- tile_holder: int32 [4, 8, 8], P('depth', 'view'), may hold values from -1 to 7, as said below
Outputs:
- image: float32 [4, 64, 4096], P(None, 'depth', 'view')
Inputs may be any that keep to these rules, and one draw needn't show every extreme that they name: Renderer (d, v) finds brick column t in slot t of holder tile_holder[d, v, t]. For fixed d and t the holders that appear are distinct over v, and the holders named by one renderer are distinct; brick column 0 is never skipped.
All inputs are finite; a program needn't handle non-finite values.
Results may differ from a plain program's by a relative error of at most 0.0003.
Values sent between devices are 32-bit elements; how exact they have to be, the bound alone decides.
No kernel may reach another device: no remote copies, remote signals or barrier semaphores. Data moves between devices by JAX's collectives and lax.ppermute only.
A program may use at most 128 MiB of HBM per device.

v0:
```python
import functools

import jax
import jax.numpy as jnp
from jax import lax
from jax.experimental import pallas as pl
from jax.experimental.pallas import tpu as pltpu
from jax.sharding import PartitionSpec as P

STEPS = 48
DENSITY = 0.8
SHARPEN = 1.5
LANES = 128
PEERS = ("depth", "view")
MARCH_BYTES = 50 * 1024 * 1024
FINISH_BYTES = 16 * 1024 * 1024
EARLY_PARTS = 2


class Plan:
    def __init__(self, depths, views, columns, edge, area):
        self.depths, self.views, self.columns = depths, views, columns
        self.pairs = area // LANES
        self.band = self.pairs // depths
        self.rows = 4 * self.band + 6
        self.peers = depths * views
        self.zts = edge // 8
        self.regs = self.pairs // 8
        self.run = min(self.regs, self.band)
        self.tops = [a for a in range(self.regs) if a % self.band == 0]
        self.bottoms = [a for a in range(self.regs) if (a + 1) % self.run == 0][-len(self.tops) :]
        self.blocks = 3 if len(self.tops) == 1 else 4

    def peer(self, depth, view):
        return depth * self.views + view

    def run_of(self, band):
        pair = band * self.band
        return pair // self.regs, pair % self.regs


def roll(x, shift, axis=1):
    return pltpu.roll(x, shift % x.shape[axis], axis)


def lane_of(shape):
    return lax.broadcasted_iota(jnp.int32, shape, 1)


def march_tile(plan, load, ready=lambda zt: None):
    scale = DENSITY / (2 * STEPS)
    regs = plan.regs
    lane = lane_of((8, LANES))
    row = lax.broadcasted_iota(jnp.int32, (8, LANES), 0)
    low = lane < 64
    inside = (lane % 64 != 0).astype(jnp.float32)
    top, bottom = row == 0, row == 7
    third = 1.0 / 3.0

    def three(zt, part):
        planes = [[load(zt, 4 * part + r, a) for a in range(regs)] for r in range(4)]
        first = [(5.0 * third) * p + third * q for p, q in zip(planes[0], planes[1])]
        second = [p + q for p, q in zip(planes[1], planes[2])]
        last = [third * p + (5.0 * third) * q for p, q in zip(planes[2], planes[3])]
        return [first, second, last]

    def step(index, behind, here, ahead, carry):
        turned = [roll(x, 64) for x in here]
        after = jnp.where(bottom, here[-1], roll(turned[0], -1, 0))
        steps_y = [y - x for x, y in zip(turned, turned[1:] + [after])]
        before = jnp.where(top, turned[0] - here[0], roll(steps_y[-1], 1, 0))
        steps_y = [before] + steps_y
        out = []
        for a in range(regs):
            total, trans, lit, red, blue = carry[a]
            x = here[a]
            grad_y = jnp.where(low, steps_y[a], steps_y[a + 1])
            diff = (x - roll(x, 1)) * inside
            grad_x = diff + roll(diff, -1)
            grad_z = ahead[a] - behind[a]
            norm = grad_x * grad_x + grad_y * grad_y + (grad_z * grad_z + 4.0)
            slope = jnp.abs(grad_z) * lax.rsqrt(norm)
            above = x - 2.0
            total = total + jnp.tanh(above)
            later = jnp.exp(total * -scale - scale * (index + 1))
            part = (trans - later) * (slope + 3.0 / 7.0)
            red = red + part * jnp.tanh(x * 0.375)
            blue = blue + part * jnp.tanh(above * 0.75)
            out.append((total, later, lit + part, red, blue))
        return out

    zero = jnp.zeros((8, LANES), jnp.float32)
    carry = [(zero, zero + 1.0, zero, zero, zero)] * regs
    samples, done = [], 0
    for zt in range(plan.zts):
        ready(zt)
        samples += three(zt, 0) + three(zt, 1)
        if zt == plan.zts - 1:
            samples.append(samples[-1])
        while done + 1 < len(samples):
            carry = step(done, samples[max(done - 1, 0)], *samples[done : done + 2], carry)
            done += 1
    value = [[], [], [], []]
    for _, trans, lit, red, blue in carry:
        value[0].append(0.35 * (lit + red))
        value[1].append(0.35 * (lit - red))
        value[2].append(0.35 * (lit + blue))
        value[3].append(1.0 - trans)
    return value


def store_tile(plan, value, tiles_ref, start):
    regs = plan.regs
    lane = lane_of((8, LANES))
    low = lane < 64
    rows = [(c // 2, c % 2 * regs + a, value[c][a]) for c in range(4) for a in range(regs)]
    spot = 0
    for a in plan.tops:
        for c in (0, 2):
            edge = jnp.where(low, value[c][a], roll(value[c + 1][a], 64))
            rows.append((2 + spot // 8, spot % 8, edge))
            spot += 1
    for a in plan.bottoms:
        for c in (0, 2):
            edge = jnp.where(low, roll(value[c][a], 64), value[c + 1][a])
            rows.append((2 + spot // 8, spot % 8, edge))
            spot += 1
    for block, at, row in rows:
        tiles_ref[block, pl.ds(start + at, 8, 8), :] = row


def store_rim(plan, value, tiles_ref, start, column, base):
    lane = lane_of((8, LANES))
    rim = jnp.zeros((8, LANES), jnp.float32)
    for c in range(4):
        for a in range(plan.regs):
            pixels = jnp.where(lane % 64 == column, value[c][a], 0.0)
            rim += roll(pixels, base + 4 * a + c - column)
    block, at = divmod(2 * len(plan.tops) + 2 * len(plan.bottoms), 8)
    tiles_ref[2 + block, pl.ds(start + at, 8, 8), :] = rim


def read_routes(plan, view, route_refs, asked_ref, order_ref):
    for i, route_ref in enumerate(route_refs):
        for r in range(2):
            found = jnp.int32(-1)
            for t in range(plan.columns):
                found = jnp.where(route_ref[r, t] == view, t, found)
            asked_ref[view ^ (plan.views - 2 - 2 * i + r)] = found
    asked = [asked_ref[v] for v in range(plan.views)]
    count = jnp.int32(0)
    for t in range(3, plan.columns):
        hit = functools.reduce(jnp.logical_or, [a == t for a in asked])
        order_ref[count + 1] = t
        count = count + jnp.where(hit, 1, 0)
    order_ref[0] = count
    return functools.reduce(jnp.logical_or, [a == 2 for a in asked])


def assemble(plan, tiles_ref, asked_ref, out_ref):
    depths, views, columns = plan.depths, plan.views, plan.columns
    regs, run, band_pairs = plan.regs, plan.run, plan.band
    lane = lane_of((1, LANES))
    zero = jnp.zeros((1, LANES), jnp.float32)
    rim_at = 2 * len(plan.tops) + 2 * len(plan.bottoms)

    def rows_of(block, slot, sublane, at, count):
        return tiles_ref[block, pl.ds(slot * 64 + sublane * 8 + at, count), :]

    asked = [asked_ref[v] for v in range(views)]

    def rim(slot, sublane):
        return rows_of(2 + rim_at // 8, slot, sublane, rim_at % 8, 1)

    def above_of(band):
        sublane, a = plan.run_of(band)
        return (sublane, a - 1) if a > 0 else (sublane - 1, regs - 1)

    def below_of(band):
        sublane, a = plan.run_of(band)
        sublane, a = sublane + (a + band_pairs) // regs, (a + band_pairs) % regs
        return sublane, a

    own, corner = {}, {}
    for slot in (0, columns - 1):
        for band in range(depths):
            sublane, a = plan.run_of(band)
            total = zero
            for i in range(band_pairs // run):
                total = total + roll(rim(slot, sublane + i), 8 * regs * i - 4 * a)
            own[slot, band] = total
            total = zero
            if band > 0:
                sublane, a = above_of(band)
                moved = roll(rim(slot, sublane), 4 * (regs - 1 - a))
                keep = (lane % (4 * regs) >= 4 * (regs - 1)) & (lane >= 64)
                total = total + jnp.where(keep, moved, 0.0)
            if band < depths - 1:
                sublane, a = below_of(band)
                moved = roll(rim(slot, sublane), -4 * a)
                keep = (lane % (4 * regs) < 4) & (lane < 64)
                total = total + jnp.where(keep, moved, 0.0)
            corner[slot, band] = total

    for v in range(views):
        slot = jnp.maximum(asked[v], 0)
        sides = []
        if v + 1 < views:
            sides.append((0, asked[v + 1] == 0))
        if v > 0:
            sides.append((columns - 1, asked[v - 1] == columns - 1))
        for band in range(depths):
            at = plan.peer(band, v) * plan.rows
            first, a = plan.run_of(band)
            for c in range(4):
                for i in range(band_pairs // run):
                    start = at + c * band_pairs + i * run
                    out_ref[pl.ds(start, run), :] = rows_of(
                        c // 2, slot, first + i, c % 2 * regs + a, run
                    )
            at += 4 * band_pairs
            above = below = jnp.zeros((2, LANES), jnp.float32)
            if band > 0:
                sublane, a = above_of(band)
                place = 2 * len(plan.tops) + 2 * plan.bottoms.index(a)
                above = rows_of(2 + place // 8, slot, sublane, place % 8, 2)
            if band < depths - 1:
                sublane, a = below_of(band)
                place = 2 * plan.tops.index(a)
                below = rows_of(2 + place // 8, slot, sublane, place % 8, 2)
            out_ref[pl.ds(at, 2), :] = above
            out_ref[pl.ds(at + 2, 2), :] = below
            out_ref[pl.ds(at + 4, 1), :] = sum(jnp.where(f, own[s, band], 0.0) for s, f in sides) + zero
            mark = jnp.where(lane == LANES - 1, asked[v].astype(jnp.float32), 0.0)
            out_ref[pl.ds(at + 5, 1), :] = sum(jnp.where(f, corner[s, band], 0.0) for s, f in sides) + mark


def fetch(plan, x_ref, slot, held, sems, place, parts):
    size = plan.zts // parts
    return [
        [
            pltpu.make_async_copy(
                x_ref.at[slot, pl.ds(part * size, size), :, a],
                held.at[place, pl.ds(part * size, size), a],
                sems.at[place, part, a],
            )
            for a in range(plan.regs)
        ]
        for part in range(parts)
    ]


def loader(plan, held, place):
    size = plan.zts * plan.regs * 64
    flat = held.reshape(held.shape[0] * size, LANES)

    def load(zt, r, a):
        return flat[pl.ds(place * size + (zt * plan.regs + a) * 64 + r, 8, 8), :]

    return load


def first_kernel(plan, x_ref, tiles_ref, next_ref, held, sems, next_sems):
    parts = fetch(plan, x_ref, 0, held, sems, 0, EARLY_PARTS)
    following = fetch(plan, x_ref, 1, next_ref, next_sems, 0, 1)
    for copies in parts + following:
        for copy in copies:
            copy.start()

    def ready(zt):
        if zt % (plan.zts // EARLY_PARTS) == 0:
            for copy in parts[zt // (plan.zts // EARLY_PARTS)]:
                copy.wait()

    value = march_tile(plan, loader(plan, held, 0), ready)
    store_tile(plan, value, tiles_ref, 0)
    store_rim(plan, value, tiles_ref, 0, 0, 0)
    for copy in following[0]:
        copy.wait()


def second_kernel(plan, x_ref, held, pair_ref, tiles_ref, next_ref, next_sems):
    following = fetch(plan, x_ref, 2, next_ref, next_sems, 0, 1)[0]
    for copy in following:
        copy.start()
    store_tile(plan, march_tile(plan, loader(plan, held, 0)), tiles_ref, 0)
    for copy in following:
        copy.wait()


def late_kernel(plan, view_ref, *refs):
    route_refs, refs = refs[: plan.views // 2], refs[plan.views // 2 :]
    early_refs, refs = refs[:2], refs[2:]
    next_ref, x_ref, out_ref, tiles_ref, held, sems, early_sems, asked_ref, order_ref = refs
    ready = [
        pltpu.make_async_copy(ref, tiles_ref.at[:, pl.ds(64 * i, 64)], early_sems.at[i])
        for i, ref in enumerate(early_refs)
    ]
    for copy in ready:
        copy.start()
    third = read_routes(plan, view_ref[0], route_refs, asked_ref, order_ref)
    count = order_ref[0]

    def copies(number):
        slot = order_ref[number + 1]
        return fetch(plan, x_ref, slot, held, sems, number % 2, 1)[0]

    @pl.when(count > 0)
    def _():
        for copy in copies(0):
            copy.start()

    @pl.when(third)
    def _():
        value = march_tile(plan, loader(plan, next_ref, 0))
        store_tile(plan, value, tiles_ref, 128)

    def step(number, carry):
        @pl.when(number + 1 < count)
        def _():
            for copy in copies(number + 1):
                copy.start()

        for copy in copies(number):
            copy.wait()
        value = march_tile(plan, loader(plan, held, number % 2))
        slot = order_ref[number + 1]
        start = pl.multiple_of(slot * 64, 64)
        store_tile(plan, value, tiles_ref, start)

        @pl.when(slot == plan.columns - 1)
        def _():
            store_rim(plan, value, tiles_ref, start, 63, 4 * plan.regs)

        return carry

    lax.fori_loop(0, count, step, 0)
    for copy in ready:
        copy.wait()
    assemble(plan, tiles_ref, asked_ref, out_ref)


SMEM = pl.BlockSpec(memory_space=pltpu.SMEM)
VMEM = pl.BlockSpec(memory_space=pltpu.VMEM)
HBM = pl.BlockSpec(memory_space=pltpu.HBM)
ANY = pl.BlockSpec(memory_space=pl.ANY)


def granted(size):
    return pltpu.CompilerParams(vmem_limit_bytes=size)


def cost(plan, bricks):
    samples = bricks * plan.pairs * LANES * STEPS
    return pl.CostEstimate(
        flops=40 * samples, bytes_accessed=6 * samples, transcendentals=5 * samples
    )


def early_results(plan):
    return dict(
        out_specs=[VMEM, VMEM],
        out_shape=[
            jax.ShapeDtypeStruct((plan.blocks, 64, LANES), jnp.float32),
            jax.ShapeDtypeStruct((1, plan.zts, plan.regs, 8, 8, LANES), jnp.float32),
        ],
        cost_estimate=cost(plan, 1),
        compiler_params=granted(MARCH_BYTES),
    )


def march_first(plan, stored):
    return pl.pallas_call(
        functools.partial(first_kernel, plan),
        in_specs=[HBM],
        scratch_shapes=[
            pltpu.VMEM((1, plan.zts, plan.regs, 8, 8, LANES), jnp.float32),
            pltpu.SemaphoreType.DMA((1, EARLY_PARTS, plan.regs)),
            pltpu.SemaphoreType.DMA((1, 1, plan.regs)),
        ],
        name="march_first",
        **early_results(plan),
    )(stored)


def march_second(plan, stored, fetched, pair):
    return pl.pallas_call(
        functools.partial(second_kernel, plan),
        in_specs=[HBM, VMEM, ANY],
        scratch_shapes=[pltpu.SemaphoreType.DMA((1, 1, plan.regs))],
        name="march_second",
        **early_results(plan),
    )(stored, fetched, pair)


def march_late(plan, view, routes, early, following, stored):
    shape = (plan.peers * plan.rows, LANES)
    return pl.pallas_call(
        functools.partial(late_kernel, plan),
        in_specs=[SMEM] + [SMEM] * len(routes) + [ANY, ANY, VMEM, HBM],
        out_specs=VMEM,
        out_shape=jax.ShapeDtypeStruct(shape, jnp.float32),
        scratch_shapes=[
            pltpu.VMEM((plan.blocks, plan.columns * 64, LANES), jnp.float32),
            pltpu.VMEM((2, plan.zts, plan.regs, 8, 8, LANES), jnp.float32),
            pltpu.SemaphoreType.DMA((2, 1, plan.regs)),
            pltpu.SemaphoreType.DMA((2,)),
            pltpu.SMEM((plan.views,), jnp.int32),
            pltpu.SMEM((plan.columns + 1,), jnp.int32),
        ],
        cost_estimate=cost(plan, plan.columns - 2),
        compiler_params=granted(MARCH_BYTES),
        name="march_late",
    )(view, *routes, *early, following, stored)


def finish_kernel(plan, source, out_ref, image, marks):
    depths, views, band, columns = plan.depths, plan.views, plan.band, plan.columns
    regs = plan.regs
    lane = lane_of((1, LANES))
    low = lane < 64

    def over(front, alpha, back):
        return front if back is None else front + (1.0 - alpha) * back

    sides = None
    lane2 = lane_of((2, LANES))
    for d in reversed(range(depths)):
        front = None
        for h in range(views):
            n = plan.peer(d, h)
            piece = source[pl.ds(n * plan.rows + 4 * band + 4, 2), :]
            front = piece if front is None else front + piece
            mark = jnp.where(lane == LANES - 1, piece[1:2], 0.0)
            mark = jnp.sum(mark, axis=1, keepdims=True)
            marks[n] = jnp.broadcast_to(mark, (8, LANES))
        alpha = front
        for c in range(3):
            alpha = jnp.where(lane2 % 4 == c, roll(front, c - 3), alpha)
        sides = over(front, alpha, sides)

    bodies, outers = [], []
    low8 = lane_of((8, LANES)) < 64
    even8 = lax.broadcasted_iota(jnp.int32, (8, LANES), 0) % 2 == 0
    for t in range(columns):
        acc, rims = [None] * 4, None
        for d in reversed(range(depths)):
            front = [jnp.zeros((band, LANES), jnp.float32)] * 4
            rim = jnp.zeros((8, LANES), jnp.float32)
            for h in range(views):
                n = plan.peer(d, h)
                at = n * plan.rows
                chosen = marks[n] == t
                front = [
                    jnp.where(chosen[:band], source[pl.ds(at + c * band, band), :], x)
                    for c, x in enumerate(front)
                ]
                rim = jnp.where(chosen, source[pl.ds(at + 4 * band - 2, 8), :], rim)
            acc = [over(f, front[3], b) for f, b in zip(front, acc)]
            alpha = jnp.where(low8, roll(rim, 64), rim)
            alpha = jnp.where(even8, roll(alpha, -1, 0), alpha)
            rims = over(rim, alpha, rims)
        bodies.append(acc)
        outers.append([[rims[2 * side + i + 2 : 2 * side + i + 3] for i in range(2)] for side in range(2)])

    count = 2 * band
    wide = lane_of((band, LANES))
    low_band = wide < 64
    number = lax.broadcasted_iota(jnp.int32, (band, LANES), 0)
    number = 8 * regs * (number // regs) + 4 * (number % regs)
    final = columns // 2 + 1
    spread = jnp.broadcast_to(sides[0:1], (band, LANES))
    for c in range(4):
        for u in range(columns // 2):
            x, y = bodies[2 * u][c], bodies[2 * u + 1][c]
            image[c, u + 1, pl.ds(8, band, 2), :] = jnp.where(low_band, x, roll(y, 64))
            image[c, u + 1, pl.ds(9, band, 2), :] = jnp.where(low_band, roll(x, 64), y)
            for side, at in ((0, 7), (1, 8 + count)):
                x, y = outers[2 * u][side][c // 2], outers[2 * u + 1][side][c // 2]
                if c % 2 == 0:
                    y = roll(y, 64)
                else:
                    x = roll(x, 64)
                image[c, u + 1, pl.ds(at, 1), :] = jnp.where(low, x, y)
        for base, tile, spot in ((0, final, 0), (4 * regs, 0, LANES - 1)):
            for odd in range(2):
                here = wide == base + 64 * odd + number + c
                column = jnp.sum(jnp.where(here, spread, 0.0), axis=1, keepdims=True)
                image[c, tile, pl.ds(8 + odd, band, 2), :] = jnp.where(wide == spot, column, 0.0)
            for at, place in ((7, 64 + base + 4 * (regs - 1) + c), (8 + count, base + c)):
                pixel = jnp.where(lane == place, sides[1:2], 0.0)
                pixel = jnp.sum(pixel, axis=1, keepdims=True)
                image[c, tile, pl.ds(at, 1), :] = jnp.where(lane == spot, pixel, 0.0)

    full = lane_of((count, LANES))
    for c in range(4):
        middle = [image[c, k, pl.ds(8, count), :] for k in range(final + 1)]
        smooth = [
            0.25 * image[c, k, pl.ds(7, count), :]
            + 0.5 * middle[k]
            + 0.25 * image[c, k, pl.ds(9, count), :]
            for k in range(final + 1)
        ]
        later = [roll(x, 1) for x in smooth]
        sooner = [roll(x, -1) for x in smooth]
        for k in range(1, final):
            left = jnp.where(full == 0, later[k - 1], later[k])
            right = jnp.where(full == LANES - 1, sooner[k + 1], sooner[k])
            blurred = 0.25 * left + 0.5 * smooth[k] + 0.25 * right
            out_ref[c, :, pl.ds((k - 1) * LANES, LANES)] = middle[k] + SHARPEN * (
                middle[k] - blurred
            )


def finish(plan, arrived):
    count = 2 * plan.band
    return pl.pallas_call(
        functools.partial(finish_kernel, plan),
        in_specs=[VMEM],
        out_specs=VMEM,
        out_shape=jax.ShapeDtypeStruct((4, count, plan.columns * 64), jnp.float32),
        scratch_shapes=[
            pltpu.VMEM((4, plan.columns // 2 + 2, count + 16, LANES), jnp.float32),
            pltpu.VMEM((plan.peers, 8, LANES), jnp.float32),
        ],
        compiler_params=granted(FINISH_BYTES),
        name="finish",
    )(arrived)


def exchange(plan, messages):
    cut = messages.reshape(plan.peers, plan.rows // 2, 2, LANES)
    moved = lax.all_to_all(cut, PEERS, split_axis=0, concat_axis=0, tiled=True)
    return moved.reshape(plan.peers * plan.rows, LANES)


def swapped(x, distance):
    pairs = [(i, i ^ distance) for i in range(lax.axis_size("view"))]
    return lax.ppermute(x, "view", pairs)


def body(bricks, tile_holder):
    depths, views = lax.axis_size("depth"), lax.axis_size("view")
    columns, edge, area = bricks.shape[2:]
    plan = Plan(depths, views, columns, edge, area)
    view = lax.axis_index("view").astype(jnp.int32).reshape(1)
    own = tile_holder.reshape(1, columns)
    pair = jnp.concatenate([own, swapped(own, 1)], axis=0)
    routes = [swapped(pair, k) for k in range(views - 2, 0, -2)] + [pair]
    stored = bricks[0, 0].reshape(columns, plan.zts, 8, plan.pairs, LANES).transpose(0, 1, 3, 2, 4)
    stored = stored.reshape(columns, plan.zts, 8, plan.regs, 8, LANES)
    first, following = march_first(plan, stored)
    second, following = march_second(plan, stored, following, pair)
    messages = march_late(plan, view, routes, (first, second), following, stored)
    return finish(plan, exchange(plan, messages))


def solution(mesh):
    in_specs = (P("depth", "view", None, None, None), P("depth", "view", None))
    out_specs = P(None, "depth", "view")
    return jax.shard_map(body, mesh=mesh, in_specs=in_specs, out_specs=out_specs, check_vma=False)
```

profile of v0, /device:TPU:0, one launch (start us, length us, event | category | flops | bytes accessed | tf_op | source)
XLA Modules:
  0.0 43.2 jit_solution(18426093039965653685)
XLA Ops:
  0.0 0.0 copy-start
  0.0 0.5 %collective-permute-start = (s32[1,8]{1,0:T(1,128)}, s32[1,8]{1,0:T(1,128)S(1)}, u32[]{:S(2)}, u32[]{:S(2)}) collective-permute-start(s32[1,8]{1,0:T(1,128)} %bitcast.14), channel_id=1, source_target_pairs={{0,1},{1,0},{2,3},{3,2},{4,5},{5,4},{6,7},{7,6},{8,9},{9,8},{10,11... | collective-permute-start | bytes 104 | tf_op jit(solution)/shard_map/ppermute | solution.py:539
  0.5 2.5 %march_first.1 = (f32[3,64,128]{2,1,0:T(8,128)S(1)}, f32[1,8,4,8,8,128]{5,4,3,2,1,0:T(8,128)S(1)}) custom-call(f32[8,8,8,4,8,128]{5,4,3,2,1,0:T(8,128)} %bitcast.11), custom_call_target="tpu_custom_call" | custom-call | flops 7864320 | bytes 1179648 | tf_op jit(solution)/shard_map/march_first/pallas_call | solution.py:373
  3.0 0.0 collective-permute-done
  3.0 0.0 copy-done
  3.0 4.7 %collective-permute-start.1 = (s32[2,8]{1,0:T(2,128)S(1)}, s32[2,8]{1,0:T(2,128)S(1)}, u32[]{:S(2)}, u32[]{:S(2)}) collective-permute-start(s32[2,8]{1,0:T(2,128)S(1)} %pad_add_fusion.pair_ref.refs_3_), channel_id=1, source_target_pairs={{0,6},{1,7},{2,4},{3,5},{4,2},{5,3},{6,0},{7,1},{8,14},{9,15},{10,... | collective-permute-start | bytes 200 | tf_op jit(solution)/shard_map/ppermute | solution.py:539
  7.7 0.0 collective-permute-start.2
  7.7 0.6 %collective-permute-start.3 = (s32[2,8]{1,0:T(2,128)S(1)}, s32[2,8]{1,0:T(2,128)S(1)}, u32[]{:S(2)}, u32[]{:S(2)}) collective-permute-start(s32[2,8]{1,0:T(2,128)S(1)} %pad_add_fusion.pair_ref.refs_3_), channel_id=1, source_target_pairs={{0,2},{1,3},{2,0},{3,1},{4,6},{5,7},{6,4},{7,5},{8,10},{9,11},{10,... | collective-permute-start | bytes 200 | tf_op jit(solution)/shard_map/ppermute | solution.py:539
  8.3 1.2 %march_second.1 = (f32[3,64,128]{2,1,0:T(8,128)S(1)}, f32[1,8,4,8,8,128]{5,4,3,2,1,0:T(8,128)S(1)}) custom-call(f32[8,8,8,4,8,128]{5,4,3,2,1,0:T(8,128)} %bitcast.12, f32[1,8,4,8,8,128]{5,4,3,2,1,0:T(8,128)S(1)} %get-tuple-element.10.held, s32[2,8]{1,0:T(2,128)S(1)} %pad_add_fusion.pair_ref.refs_3_), custom_call_target="tpu_custom_call" | custom-call | flops 7864320 | bytes 1179648 | tf_op jit(solution)/shard_map/march_second/pallas_call | solution.py:387
  9.6 0.0 collective-permute-done.1.refs_0_
  9.6 2.6 %collective-permute-done.2.refs_1_ = s32[2,8]{1,0:T(2,128)S(1)} collective-permute-done((s32[2,8]{1,0:T(2,128)S(1)}, s32[2,8]{1,0:T(2,128)S(1)}, u32[]{:S(2)}, u32[]{:S(2)}) %collective-permute-start.2) | collective-permute-done | bytes 96 | tf_op jit(solution)/shard_map/ppermute | solution.py:539
  12.2 0.0 collective-permute-done.3.refs_2_
  12.2 4.6 %march_late.1 = f32[1216,128]{1,0:T(8,128)S(1)} custom-call(s32[1]{0:T(128)} %bitcast.view_ref, s32[2,8]{1,0:T(2,128)S(1)} %collective-permute-done.1.refs_0_, s32[2,8]{1,0:T(2,128)S(1)} %collective-permute-done.2.refs_1_, s32[2,8]{1,0:T(2,128)S(1)} %collective-permute-done.3.refs_2_, s32[2,8]{1,0:T(2,128)S(1)} %pad_add_fusion.pair_ref.refs_3_, ...), custom_call_target="tpu_custom_call" | custom-call | flops 47185920 | bytes 7077888 | tf_op jit(solution)/shard_map/march_late/pallas_call | solution.py:398
  16.8 25.0 %all_to_all.5 = f32[32,19,2,128]{3,2,1,0:T(2,128)S(1)} all-to-all(f32[32,19,2,128]{3,2,1,0:T(2,128)S(1)} %bitcast.10), channel_id=1, replica_groups=mesh['depth'=4,'view'=8] {'depth','view'}, dimensions={0} | all-to-all | bytes 1245184 | tf_op jit(solution)/shard_map/all_to_all | solution.py:533
  41.8 1.4 %finish.1 = f32[4,16,512]{2,1,0:T(8,128)} custom-call(f32[1216,128]{1,0:T(8,128)S(1)} %bitcast.9), custom_call_target="tpu_custom_call" | custom-call | tf_op jit(solution)/shard_map/finish/pallas_call | solution.py:517
  (1 shorter events, 0.0 us)
Async XLA Ops:
  0.0 3.0 %copy-start = (s32[1,1,8]{2,1,0:T(1,128)S(1)}, s32[1,1,8]{2,1,0:T(1,128)}, u32[]{:S(2)}) copy-start(s32[1,1,8]{2,1,0:T(1,128)} %param.3) | copy-start | bytes 100
  0.0 3.0 %collective-permute-start = (s32[1,8]{1,0:T(1,128)}, s32[1,8]{1,0:T(1,128)S(1)}, u32[]{:S(2)}, u32[]{:S(2)}) collective-permute-start(s32[1,8]{1,0:T(1,128)} %bitcast.14), channel_id=1, source_target_pairs={{0,1},{1,0},{2,3},{3,2},{4,5},{5,4},{6,7},{7,6},{8,9},{9,8},{10,11... | collective-permute-start | bytes 104 | tf_op jit(solution)/shard_map/ppermute | solution.py:539
  3.0 6.6 %collective-permute-start.1 = (s32[2,8]{1,0:T(2,128)S(1)}, s32[2,8]{1,0:T(2,128)S(1)}, u32[]{:S(2)}, u32[]{:S(2)}) collective-permute-start(s32[2,8]{1,0:T(2,128)S(1)} %pad_add_fusion.pair_ref.refs_3_), channel_id=1, source_target_pairs={{0,6},{1,7},{2,4},{3,5},{4,2},{5,3},{6,0},{7,1},{8,14},{9,15},{10,... | collective-permute-start | bytes 200 | tf_op jit(solution)/shard_map/ppermute | solution.py:539
  7.7 4.5 %collective-permute-start.2 = (s32[2,8]{1,0:T(2,128)S(1)}, s32[2,8]{1,0:T(2,128)S(1)}, u32[]{:S(2)}, u32[]{:S(2)}) collective-permute-start(s32[2,8]{1,0:T(2,128)S(1)} %pad_add_fusion.pair_ref.refs_3_), channel_id=1, source_target_pairs={{0,4},{1,5},{2,6},{3,7},{4,0},{5,1},{6,2},{7,3},{8,12},{9,13},{10,... | collective-permute-start | bytes 200 | tf_op jit(solution)/shard_map/ppermute | solution.py:539
  7.7 4.5 %collective-permute-start.3 = (s32[2,8]{1,0:T(2,128)S(1)}, s32[2,8]{1,0:T(2,128)S(1)}, u32[]{:S(2)}, u32[]{:S(2)}) collective-permute-start(s32[2,8]{1,0:T(2,128)S(1)} %pad_add_fusion.pair_ref.refs_3_), channel_id=1, source_target_pairs={{0,2},{1,3},{2,0},{3,1},{4,6},{5,7},{6,4},{7,5},{8,10},{9,11},{10,... | collective-permute-start | bytes 200 | tf_op jit(solution)/shard_map/ppermute | solution.py:539
where the time goes:
time: 43.2 us
  blocking collectives  25 us (58%)
  Pallas kernels  9.79 us (23%)
  starting transfers between devices  5.77 us (13%)
  waiting for transfers between devices  2.57 us (6%)
    all_to_all x1, blocking collectives, exchange(): moved = lax.all_to_all(cut, PEERS, split_axis=0, concat_axis=0, tiled=True)  25 us
    ppermute x4, starting transfers between devices, swapped(): return lax.ppermute(x, 'view', pairs)  5.77 us
    pallas_call x1, Pallas kernels, march_late(): pl.pallas_call(functools.partial(late_kernel, plan), in_specs=[SMEM] + [S...  4.61 us
    ppermute x4, waiting for transfers between devices, swapped(): return lax.ppermute(x, 'view', pairs)  2.57 us
    pallas_call x1, Pallas kernels, march_first(): pl.pallas_call(functools.partial(first_kernel, plan), in_specs=[HBM], scr...  2.53 us
    pallas_call x1, Pallas kernels, finish(): pl.pallas_call(functools.partial(finish_kernel, plan), in_specs=[VMEM], o...  1.4 us
    pallas_call x1, Pallas kernels, march_second(): pl.pallas_call(functools.partial(second_kernel, plan), in_specs=[HBM, VME...  1.24 us
  transfers between devices with their start and end apart: 4, of which 1 were waited for; matrix products, arithmetic and copies ran while one was open for 0% of the time, Pallas kernels for 9%

commit v1 on v0

--- a/solution.py
+++ b/solution.py
@@ -414,7 +414,7 @@
     )(view, *routes, *early, following, stored)
 
 
-def finish_kernel(plan, source, out_ref, image, marks):
+def finish_kernel(plan, source, out_ref, image, sender_ref):
     depths, views, band, columns = plan.depths, plan.views, plan.band, plan.columns
     regs = plan.regs
     lane = lane_of((1, LANES))
@@ -423,6 +423,9 @@
     def over(front, alpha, back):
         return front if back is None else front + (1.0 - alpha) * back
 
+    for d in range(depths):
+        for t in range(columns):
+            sender_ref[d, t] = -1
     sides = None
     lane2 = lane_of((2, LANES))
     for d in reversed(range(depths)):
@@ -432,8 +435,8 @@
             piece = source[pl.ds(n * plan.rows + 4 * band + 4, 2), :]
             front = piece if front is None else front + piece
             mark = jnp.where(lane == LANES - 1, piece[1:2], 0.0)
-            mark = jnp.sum(mark, axis=1, keepdims=True)
-            marks[n] = jnp.broadcast_to(mark, (8, LANES))
+            mark = jnp.sum(mark).astype(jnp.int32)
+            sender_ref[d, jnp.where(mark >= 0, mark, columns)] = n
         alpha = front
         for c in range(3):
             alpha = jnp.where(lane2 % 4 == c, roll(front, c - 3), alpha)
@@ -445,17 +448,13 @@
     for t in range(columns):
         acc, rims = [None] * 4, None
         for d in reversed(range(depths)):
-            front = [jnp.zeros((band, LANES), jnp.float32)] * 4
-            rim = jnp.zeros((8, LANES), jnp.float32)
-            for h in range(views):
-                n = plan.peer(d, h)
-                at = n * plan.rows
-                chosen = marks[n] == t
-                front = [
-                    jnp.where(chosen[:band], source[pl.ds(at + c * band, band), :], x)
-                    for c, x in enumerate(front)
-                ]
-                rim = jnp.where(chosen, source[pl.ds(at + 4 * band - 2, 8), :], rim)
+            n = sender_ref[d, t]
+            at = jnp.maximum(n, 0) * plan.rows
+            shown = n >= 0
+            front = [
+                jnp.where(shown, source[pl.ds(at + c * band, band), :], 0.0) for c in range(4)
+            ]
+            rim = jnp.where(shown, source[pl.ds(at + 4 * band - 2, 8), :], 0.0)
             acc = [over(f, front[3], b) for f, b in zip(front, acc)]
             alpha = jnp.where(low8, roll(rim, 64), rim)
             alpha = jnp.where(even8, roll(alpha, -1, 0), alpha)
@@ -521,7 +520,7 @@
         out_shape=jax.ShapeDtypeStruct((4, count, plan.columns * 64), jnp.float32),
         scratch_shapes=[
             pltpu.VMEM((4, plan.columns // 2 + 2, count + 16, LANES), jnp.float32),
-            pltpu.VMEM((plan.peers, 8, LANES), jnp.float32),
+            pltpu.SMEM((plan.depths, plan.columns + 1), jnp.int32),
         ],
         compiler_params=granted(FINISH_BYTES),
         name="finish",

time: 43.2 us -> 41.7 us (0.965); the launches traced: 43.2 us -> 41 us
  Pallas kernels: 9.79 us -> 7.36 us
    pallas_call x1, Pallas kernels: 4.61 us -> 2.22 us  [march_late(): pl.pallas_call(functools.partial(late_kernel, plan), in_specs=[SMEM] + [S...]
where the time goes in v1:
time: 41.7 us; the launch traced here: 41 us
  blocking collectives  25.3 us (61%)
  Pallas kernels  7.36 us (18%)
  starting transfers between devices  5.77 us (14%)
  waiting for transfers between devices  2.57 us (6%)
    all_to_all x1, blocking collectives, exchange(): moved = lax.all_to_all(cut, PEERS, split_axis=0, concat_axis=0, tiled=True)  25.3 us
    ppermute x4, starting transfers between devices, swapped(): return lax.ppermute(x, 'view', pairs)  5.77 us
    ppermute x4, waiting for transfers between devices, swapped(): return lax.ppermute(x, 'view', pairs)  2.57 us
    pallas_call x1, Pallas kernels, march_first(): pl.pallas_call(functools.partial(first_kernel, plan), in_specs=[HBM], scr...  2.53 us
    pallas_call x1, Pallas kernels, march_late(): pl.pallas_call(functools.partial(late_kernel, plan), in_specs=[SMEM] + [S...  2.22 us
    pallas_call x1, Pallas kernels, finish(): pl.pallas_call(functools.partial(finish_kernel, plan), in_specs=[VMEM], o...  1.37 us
    pallas_call x1, Pallas kernels, march_second(): pl.pallas_call(functools.partial(second_kernel, plan), in_specs=[HBM, VME...  1.24 us
  transfers between devices with their start and end apart: 4, of which 1 were waited for; matrix products, arithmetic and copies ran while one was open for 0% of the time, Pallas kernels for 9%

profile of v1, /device:TPU:0, one launch (start us, length us, event | category | flops | bytes accessed | tf_op | source)
XLA Modules:
  0.0 41.0 jit_solution(909652086525131136)
XLA Ops:
  0.0 0.0 copy-start
  0.0 0.5 %collective-permute-start = (s32[1,8]{1,0:T(1,128)}, s32[1,8]{1,0:T(1,128)S(1)}, u32[]{:S(2)}, u32[]{:S(2)}) collective-permute-start(s32[1,8]{1,0:T(1,128)} %bitcast.14), channel_id=1, source_target_pairs={{0,1},{1,0},{2,3},{3,2},{4,5},{5,4},{6,7},{7,6},{8,9},{9,8},{10,11... | collective-permute-start | bytes 104 | tf_op jit(solution)/shard_map/ppermute | solution.py:538
  0.5 2.5 %march_first.1 = (f32[3,64,128]{2,1,0:T(8,128)S(1)}, f32[1,8,4,8,8,128]{5,4,3,2,1,0:T(8,128)S(1)}) custom-call(f32[8,8,8,4,8,128]{5,4,3,2,1,0:T(8,128)} %bitcast.11), custom_call_target="tpu_custom_call" | custom-call | flops 7864320 | bytes 1179648 | tf_op jit(solution)/shard_map/march_first/pallas_call | solution.py:373
  3.0 0.0 collective-permute-done
  3.0 0.0 copy-done
  3.0 4.7 %collective-permute-start.1 = (s32[2,8]{1,0:T(2,128)S(1)}, s32[2,8]{1,0:T(2,128)S(1)}, u32[]{:S(2)}, u32[]{:S(2)}) collective-permute-start(s32[2,8]{1,0:T(2,128)S(1)} %pad_add_fusion.pair_ref.refs_3_), channel_id=1, source_target_pairs={{0,6},{1,7},{2,4},{3,5},{4,2},{5,3},{6,0},{7,1},{8,14},{9,15},{10,... | collective-permute-start | bytes 200 | tf_op jit(solution)/shard_map/ppermute | solution.py:538
  7.7 0.0 collective-permute-start.2
  7.7 0.6 %collective-permute-start.3 = (s32[2,8]{1,0:T(2,128)S(1)}, s32[2,8]{1,0:T(2,128)S(1)}, u32[]{:S(2)}, u32[]{:S(2)}) collective-permute-start(s32[2,8]{1,0:T(2,128)S(1)} %pad_add_fusion.pair_ref.refs_3_), channel_id=1, source_target_pairs={{0,2},{1,3},{2,0},{3,1},{4,6},{5,7},{6,4},{7,5},{8,10},{9,11},{10,... | collective-permute-start | bytes 200 | tf_op jit(solution)/shard_map/ppermute | solution.py:538
  8.3 1.2 %march_second.1 = (f32[3,64,128]{2,1,0:T(8,128)S(1)}, f32[1,8,4,8,8,128]{5,4,3,2,1,0:T(8,128)S(1)}) custom-call(f32[8,8,8,4,8,128]{5,4,3,2,1,0:T(8,128)} %bitcast.12, f32[1,8,4,8,8,128]{5,4,3,2,1,0:T(8,128)S(1)} %get-tuple-element.10.held, s32[2,8]{1,0:T(2,128)S(1)} %pad_add_fusion.pair_ref.refs_3_), custom_call_target="tpu_custom_call" | custom-call | flops 7864320 | bytes 1179648 | tf_op jit(solution)/shard_map/march_second/pallas_call | solution.py:387
  9.6 0.0 collective-permute-done.1.refs_0_
  9.6 2.6 %collective-permute-done.2.refs_1_ = s32[2,8]{1,0:T(2,128)S(1)} collective-permute-done((s32[2,8]{1,0:T(2,128)S(1)}, s32[2,8]{1,0:T(2,128)S(1)}, u32[]{:S(2)}, u32[]{:S(2)}) %collective-permute-start.2) | collective-permute-done | bytes 96 | tf_op jit(solution)/shard_map/ppermute | solution.py:538
  12.2 0.0 collective-permute-done.3.refs_2_
  12.2 2.2 %march_late.1 = f32[1216,128]{1,0:T(8,128)S(1)} custom-call(s32[1]{0:T(128)} %bitcast.view_ref, s32[2,8]{1,0:T(2,128)S(1)} %collective-permute-done.1.refs_0_, s32[2,8]{1,0:T(2,128)S(1)} %collective-permute-done.2.refs_1_, s32[2,8]{1,0:T(2,128)S(1)} %collective-permute-done.3.refs_2_, s32[2,8]{1,0:T(2,128)S(1)} %pad_add_fusion.pair_ref.refs_3_, ...), custom_call_target="tpu_custom_call" | custom-call | flops 47185920 | bytes 7077888 | tf_op jit(solution)/shard_map/march_late/pallas_call | solution.py:398
  14.4 25.3 %all_to_all.5 = f32[32,19,2,128]{3,2,1,0:T(2,128)S(1)} all-to-all(f32[32,19,2,128]{3,2,1,0:T(2,128)S(1)} %bitcast.10), channel_id=1, replica_groups=mesh['depth'=4,'view'=8] {'depth','view'}, dimensions={0} | all-to-all | bytes 1245184 | tf_op jit(solution)/shard_map/all_to_all | solution.py:532
  39.7 1.4 %finish.1 = f32[4,16,512]{2,1,0:T(8,128)} custom-call(f32[1216,128]{1,0:T(8,128)S(1)} %bitcast.9), custom_call_target="tpu_custom_call" | custom-call | tf_op jit(solution)/shard_map/finish/pallas_call | solution.py:516
  (1 shorter events, 0.0 us)
Async XLA Ops:
  0.0 3.0 %copy-start = (s32[1,1,8]{2,1,0:T(1,128)S(1)}, s32[1,1,8]{2,1,0:T(1,128)}, u32[]{:S(2)}) copy-start(s32[1,1,8]{2,1,0:T(1,128)} %param.3) | copy-start | bytes 100
  0.0 3.0 %collective-permute-start = (s32[1,8]{1,0:T(1,128)}, s32[1,8]{1,0:T(1,128)S(1)}, u32[]{:S(2)}, u32[]{:S(2)}) collective-permute-start(s32[1,8]{1,0:T(1,128)} %bitcast.14), channel_id=1, source_target_pairs={{0,1},{1,0},{2,3},{3,2},{4,5},{5,4},{6,7},{7,6},{8,9},{9,8},{10,11... | collective-permute-start | bytes 104 | tf_op jit(solution)/shard_map/ppermute | solution.py:538
  3.0 6.6 %collective-permute-start.1 = (s32[2,8]{1,0:T(2,128)S(1)}, s32[2,8]{1,0:T(2,128)S(1)}, u32[]{:S(2)}, u32[]{:S(2)}) collective-permute-start(s32[2,8]{1,0:T(2,128)S(1)} %pad_add_fusion.pair_ref.refs_3_), channel_id=1, source_target_pairs={{0,6},{1,7},{2,4},{3,5},{4,2},{5,3},{6,0},{7,1},{8,14},{9,15},{10,... | collective-permute-start | bytes 200 | tf_op jit(solution)/shard_map/ppermute | solution.py:538
  7.7 4.5 %collective-permute-start.2 = (s32[2,8]{1,0:T(2,128)S(1)}, s32[2,8]{1,0:T(2,128)S(1)}, u32[]{:S(2)}, u32[]{:S(2)}) collective-permute-start(s32[2,8]{1,0:T(2,128)S(1)} %pad_add_fusion.pair_ref.refs_3_), channel_id=1, source_target_pairs={{0,4},{1,5},{2,6},{3,7},{4,0},{5,1},{6,2},{7,3},{8,12},{9,13},{10,... | collective-permute-start | bytes 200 | tf_op jit(solution)/shard_map/ppermute | solution.py:538
  7.7 4.5 %collective-permute-start.3 = (s32[2,8]{1,0:T(2,128)S(1)}, s32[2,8]{1,0:T(2,128)S(1)}, u32[]{:S(2)}, u32[]{:S(2)}) collective-permute-start(s32[2,8]{1,0:T(2,128)S(1)} %pad_add_fusion.pair_ref.refs_3_), channel_id=1, source_target_pairs={{0,2},{1,3},{2,0},{3,1},{4,6},{5,7},{6,4},{7,5},{8,10},{9,11},{10,... | collective-permute-start | bytes 200 | tf_op jit(solution)/shard_map/ppermute | solution.py:538

commit v2 on v1

--- a/solution.py
+++ b/solution.py
@@ -24,6 +24,7 @@
         self.band = self.pairs // depths
         self.rows = 4 * self.band + 6
         self.peers = depths * views
+        self.hops = sorted(range(2, views, 2), key=lambda k: -(k ^ 2))
         self.zts = edge // 8
         self.regs = self.pairs // 8
         self.run = min(self.regs, self.band)
@@ -146,7 +147,7 @@
             found = jnp.int32(-1)
             for t in range(plan.columns):
                 found = jnp.where(route_ref[r, t] == view, t, found)
-            asked_ref[view ^ (plan.views - 2 - 2 * i + r)] = found
+            asked_ref[view ^ ((plan.hops + [0])[i] + r)] = found
     asked = [asked_ref[v] for v in range(plan.views)]
     count = jnp.int32(0)
     for t in range(3, plan.columns):
@@ -545,7 +546,7 @@
     view = lax.axis_index("view").astype(jnp.int32).reshape(1)
     own = tile_holder.reshape(1, columns)
     pair = jnp.concatenate([own, swapped(own, 1)], axis=0)
-    routes = [swapped(pair, k) for k in range(views - 2, 0, -2)] + [pair]
+    routes = [swapped(pair, k) for k in plan.hops] + [pair]
     stored = bricks[0, 0].reshape(columns, plan.zts, 8, plan.pairs, LANES).transpose(0, 1, 3, 2, 4)
     stored = stored.reshape(columns, plan.zts, 8, plan.regs, 8, LANES)
     first, following = march_first(plan, stored)

time: 41.7 us -> 42 us (level); the launches traced: 41 us -> 41.8 us
  Pallas kernels: 7.36 us -> 8.56 us
    pallas_call x1, Pallas kernels: 2.22 us -> 3.42 us  [march_late(): pl.pallas_call(functools.partial(late_kernel, plan), in_specs=[SMEM] + [S...]
where the time goes in v2:
time: 42 us; the launch traced here: 41.8 us
  blocking collectives  24.9 us (59%)
  Pallas kernels  8.56 us (20%)
  starting transfers between devices  5.69 us (14%)
  waiting for transfers between devices  2.54 us (6%)
    all_to_all x1, blocking collectives, exchange(): moved = lax.all_to_all(cut, PEERS, split_axis=0, concat_axis=0, tiled=True)  24.9 us
    ppermute x4, starting transfers between devices, swapped(): return lax.ppermute(x, 'view', pairs)  5.69 us
    pallas_call x1, Pallas kernels, march_late(): pl.pallas_call(functools.partial(late_kernel, plan), in_specs=[SMEM] + [S...  3.42 us
    ppermute x4, waiting for transfers between devices, swapped(): return lax.ppermute(x, 'view', pairs)  2.54 us
    pallas_call x1, Pallas kernels, march_first(): pl.pallas_call(functools.partial(first_kernel, plan), in_specs=[HBM], scr...  2.53 us
    pallas_call x1, Pallas kernels, finish(): pl.pallas_call(functools.partial(finish_kernel, plan), in_specs=[VMEM], o...  1.37 us
    pallas_call x1, Pallas kernels, march_second(): pl.pallas_call(functools.partial(second_kernel, plan), in_specs=[HBM, VME...  1.24 us
  transfers between devices with their start and end apart: 4, of which 1 were waited for; matrix products, arithmetic and copies ran while one was open for 0% of the time, Pallas kernels for 9%

profile of v2, /device:TPU:0, one launch (start us, length us, event | category | flops | bytes accessed | tf_op | source)
XLA Modules:
  0.0 41.8 jit_solution(1062065583500558729)
XLA Ops:
  0.0 0.0 copy-start
  0.0 0.5 %collective-permute-start = (s32[1,8]{1,0:T(1,128)}, s32[1,8]{1,0:T(1,128)S(1)}, u32[]{:S(2)}, u32[]{:S(2)}) collective-permute-start(s32[1,8]{1,0:T(1,128)} %bitcast.14), channel_id=1, source_target_pairs={{0,1},{1,0},{2,3},{3,2},{4,5},{5,4},{6,7},{7,6},{8,9},{9,8},{10,11... | collective-permute-start | bytes 104 | tf_op jit(solution)/shard_map/ppermute | solution.py:539
  0.5 2.5 %march_first.1 = (f32[3,64,128]{2,1,0:T(8,128)S(1)}, f32[1,8,4,8,8,128]{5,4,3,2,1,0:T(8,128)S(1)}) custom-call(f32[8,8,8,4,8,128]{5,4,3,2,1,0:T(8,128)} %bitcast.11), custom_call_target="tpu_custom_call" | custom-call | flops 7864320 | bytes 1179648 | tf_op jit(solution)/shard_map/march_first/pallas_call | solution.py:374
  3.0 0.0 collective-permute-done
  3.0 0.0 copy-done
  3.0 3.7 %collective-permute-start.1 = (s32[2,8]{1,0:T(2,128)S(1)}, s32[2,8]{1,0:T(2,128)S(1)}, u32[]{:S(2)}, u32[]{:S(2)}) collective-permute-start(s32[2,8]{1,0:T(2,128)S(1)} %pad_add_fusion.pair_ref.refs_3_), channel_id=1, source_target_pairs={{0,4},{1,5},{2,6},{3,7},{4,0},{5,1},{6,2},{7,3},{8,12},{9,13},{10,... | collective-permute-start | bytes 200 | tf_op jit(solution)/shard_map/ppermute | solution.py:539
  6.7 1.3 %collective-permute-start.2 = (s32[2,8]{1,0:T(2,128)S(1)}, s32[2,8]{1,0:T(2,128)S(1)}, u32[]{:S(2)}, u32[]{:S(2)}) collective-permute-start(s32[2,8]{1,0:T(2,128)S(1)} %pad_add_fusion.pair_ref.refs_3_), channel_id=1, source_target_pairs={{0,6},{1,7},{2,4},{3,5},{4,2},{5,3},{6,0},{7,1},{8,14},{9,15},{10,... | collective-permute-start | bytes 200 | tf_op jit(solution)/shard_map/ppermute | solution.py:539
  8.0 0.2 collective-permute-start.3
  8.3 1.2 %march_second.1 = (f32[3,64,128]{2,1,0:T(8,128)S(1)}, f32[1,8,4,8,8,128]{5,4,3,2,1,0:T(8,128)S(1)}) custom-call(f32[8,8,8,4,8,128]{5,4,3,2,1,0:T(8,128)} %bitcast.12, f32[1,8,4,8,8,128]{5,4,3,2,1,0:T(8,128)S(1)} %get-tuple-element.10.held, s32[2,8]{1,0:T(2,128)S(1)} %pad_add_fusion.pair_ref.refs_3_), custom_call_target="tpu_custom_call" | custom-call | flops 7864320 | bytes 1179648 | tf_op jit(solution)/shard_map/march_second/pallas_call | solution.py:388
  9.5 0.0 collective-permute-done.1.refs_0_
  9.5 2.5 %collective-permute-done.2.refs_1_ = s32[2,8]{1,0:T(2,128)S(1)} collective-permute-done((s32[2,8]{1,0:T(2,128)S(1)}, s32[2,8]{1,0:T(2,128)S(1)}, u32[]{:S(2)}, u32[]{:S(2)}) %collective-permute-start.2) | collective-permute-done | bytes 96 | tf_op jit(solution)/shard_map/ppermute | solution.py:539
  12.1 0.0 collective-permute-done.3.refs_2_
  12.1 3.4 %march_late.1 = f32[1216,128]{1,0:T(8,128)S(1)} custom-call(s32[1]{0:T(128)} %bitcast.view_ref, s32[2,8]{1,0:T(2,128)S(1)} %collective-permute-done.1.refs_0_, s32[2,8]{1,0:T(2,128)S(1)} %collective-permute-done.2.refs_1_, s32[2,8]{1,0:T(2,128)S(1)} %collective-permute-done.3.refs_2_, s32[2,8]{1,0:T(2,128)S(1)} %pad_add_fusion.pair_ref.refs_3_, ...), custom_call_target="tpu_custom_call" | custom-call | flops 47185920 | bytes 7077888 | tf_op jit(solution)/shard_map/march_late/pallas_call | solution.py:399
  15.5 24.9 %all_to_all.5 = f32[32,19,2,128]{3,2,1,0:T(2,128)S(1)} all-to-all(f32[32,19,2,128]{3,2,1,0:T(2,128)S(1)} %bitcast.10), channel_id=1, replica_groups=mesh['depth'=4,'view'=8] {'depth','view'}, dimensions={0} | all-to-all | bytes 1245184 | tf_op jit(solution)/shard_map/all_to_all | solution.py:533
  40.4 1.4 %finish.1 = f32[4,16,512]{2,1,0:T(8,128)} custom-call(f32[1216,128]{1,0:T(8,128)S(1)} %bitcast.9), custom_call_target="tpu_custom_call" | custom-call | tf_op jit(solution)/shard_map/finish/pallas_call | solution.py:517
  (1 shorter events, 0.0 us)
Async XLA Ops:
  0.0 3.0 %copy-start = (s32[1,1,8]{2,1,0:T(1,128)S(1)}, s32[1,1,8]{2,1,0:T(1,128)}, u32[]{:S(2)}) copy-start(s32[1,1,8]{2,1,0:T(1,128)} %param.3) | copy-start | bytes 100
  0.0 3.0 %collective-permute-start = (s32[1,8]{1,0:T(1,128)}, s32[1,8]{1,0:T(1,128)S(1)}, u32[]{:S(2)}, u32[]{:S(2)}) collective-permute-start(s32[1,8]{1,0:T(1,128)} %bitcast.14), channel_id=1, source_target_pairs={{0,1},{1,0},{2,3},{3,2},{4,5},{5,4},{6,7},{7,6},{8,9},{9,8},{10,11... | collective-permute-start | bytes 104 | tf_op jit(solution)/shard_map/ppermute | solution.py:539
  3.0 6.5 %collective-permute-start.1 = (s32[2,8]{1,0:T(2,128)S(1)}, s32[2,8]{1,0:T(2,128)S(1)}, u32[]{:S(2)}, u32[]{:S(2)}) collective-permute-start(s32[2,8]{1,0:T(2,128)S(1)} %pad_add_fusion.pair_ref.refs_3_), channel_id=1, source_target_pairs={{0,4},{1,5},{2,6},{3,7},{4,0},{5,1},{6,2},{7,3},{8,12},{9,13},{10,... | collective-permute-start | bytes 200 | tf_op jit(solution)/shard_map/ppermute | solution.py:539
  6.7 5.4 %collective-permute-start.2 = (s32[2,8]{1,0:T(2,128)S(1)}, s32[2,8]{1,0:T(2,128)S(1)}, u32[]{:S(2)}, u32[]{:S(2)}) collective-permute-start(s32[2,8]{1,0:T(2,128)S(1)} %pad_add_fusion.pair_ref.refs_3_), channel_id=1, source_target_pairs={{0,6},{1,7},{2,4},{3,5},{4,2},{5,3},{6,0},{7,1},{8,14},{9,15},{10,... | collective-permute-start | bytes 200 | tf_op jit(solution)/shard_map/ppermute | solution.py:539
  8.0 4.0 %collective-permute-start.3 = (s32[2,8]{1,0:T(2,128)S(1)}, s32[2,8]{1,0:T(2,128)S(1)}, u32[]{:S(2)}, u32[]{:S(2)}) collective-permute-start(s32[2,8]{1,0:T(2,128)S(1)} %pad_add_fusion.pair_ref.refs_3_), channel_id=1, source_target_pairs={{0,2},{1,3},{2,0},{3,1},{4,6},{5,7},{6,4},{7,5},{8,10},{9,11},{10,... | collective-permute-start | bytes 200 | tf_op jit(solution)/shard_map/ppermute | solution.py:539
